TPU v7x, 32 devices: a whole 2x2x4 slice. The times are simulated.
32 devices in a mesh: tm: 8 (over z, y), space: 4 (over x, core).
Axes of the slice: x: 2, y: 2, z: 4, core: 2. Of those that a mesh axis runs over, the one named last changes fastest.
Arguments:
- snapshots: bfloat16 [4096, 3, 4096], P('tm', None, 'space'), may hold values from -6 to 6
- cell_weights: float32 [4096], P('space'), may hold values from 0.25 to 4
- triads: int32 [64, 3], replicated, may hold values from 0 to 127, as said below
- owner_slots: int32 [8, 16], replicated, may hold values from -1 to 63, as said below
Outputs:
- bispectra: float32 [128, 512], P(('tm', 'space'))
Inputs may be any that keep to these rules, and one draw needn't show every extreme that they name: `triads`: every row is (k, l, k + l); all three entries are below 128. `owner_slots`: every triad index stands in exactly one slot of the table; in each row the used slots come first and the others hold -1; some owner fills all 16 slots.
All inputs are finite; a program needn't handle non-finite values.
Results may differ from a plain program's by a relative error of at most 0.0076.
Values may be sent and summed in bfloat16 or wider, within the bound.
A program may use at most 64 MiB of HBM per device.

v0:
```python
import math

import jax
import jax.numpy as jnp
from jax import lax
from jax.sharding import PartitionSpec as P

NB = 16
NT = 256
K = 128


def spectral_table():
    sample = jnp.arange(NT, dtype=jnp.int32)
    freq_bins = jnp.arange(K, dtype=jnp.int32)
    phase_idx = freq_bins[:, None] * sample[None, :] % NT
    angles = 2.0 * math.pi / NT * phase_idx.astype(jnp.float32)
    window = 0.5 - 0.5 * jnp.cos(2.0 * math.pi / NT * sample.astype(jnp.float32))
    norm_scale = math.sqrt(8.0 / (3.0 * NT))
    real_rows = norm_scale * window[None, :] * jnp.cos(angles)
    imag_rows = -norm_scale * window[None, :] * jnp.sin(angles)
    return jnp.stack([real_rows, imag_rows], axis=1).reshape(2 * K, NT).astype(jnp.bfloat16)


def transform(piece):
    snap_total, item_count, cell_count = piece.shape
    blocks = piece.reshape(NB, NT, item_count * cell_count)
    spectra = jnp.einsum(
        "jn,bnc->jbc", spectral_table(), blocks, preferred_element_type=jnp.float32
    )
    return spectra.astype(jnp.bfloat16).reshape(K, 2, NB, item_count, cell_count)


def triad_terms(spectra, weight_rows, triads, triad_index):
    count = triad_index.shape[0]
    lane_total = weight_rows.shape[0]
    triad_freqs = jnp.take(triads, triad_index, axis=0)
    first_spec = (
        jnp.take(spectra, triad_freqs[:, 0], axis=0)
        .reshape(count, 2, NB, lane_total)
        .astype(jnp.float32)
    )
    second_spec = (
        jnp.take(spectra, triad_freqs[:, 1], axis=0)
        .reshape(count, 2, NB, lane_total)
        .astype(jnp.float32)
    )
    third_spec = jnp.take(spectra, triad_freqs[:, 2], axis=0).reshape(count, 2, NB, lane_total)
    prod_real = (
        first_spec[:, 0] * second_spec[:, 0] - first_spec[:, 1] * second_spec[:, 1]
    ) * weight_rows
    prod_imag = (
        first_spec[:, 0] * second_spec[:, 1] + first_spec[:, 1] * second_spec[:, 0]
    ) * weight_rows
    product = jnp.stack([prod_real, prod_imag], axis=1).astype(jnp.bfloat16)
    gram = jnp.einsum("trbc,tsdc->trbsd", product, third_spec, preferred_element_type=jnp.float32)
    bis_real = gram[:, 0, :, 0, :] + gram[:, 1, :, 1, :]
    bis_imag = gram[:, 0, :, 1, :] - gram[:, 1, :, 0, :]
    return jnp.stack([bis_real, bis_imag], axis=1).reshape(count, 2 * NB * NB)


def block_size(amount, quantum):
    return quantum * math.gcd(amount // quantum, max(1, 64 // quantum))


def blocked(index_list, quantum, spectra, weight_rows, triads):
    amount = index_list.shape[0]
    width_blk = block_size(amount, quantum)
    grouped = index_list.reshape(amount // width_blk, width_blk)

    def group_terms(slot_group):
        filled = (slot_group >= 0).astype(jnp.float32)
        return (
            triad_terms(spectra, weight_rows, triads, jnp.maximum(slot_group, 0)) * filled[:, None]
        )

    return lax.map(group_terms, grouped).reshape(amount, 2 * NB * NB)


def shards(snapshots, cell_weights, triads, owner_slots):
    spectra = transform(lax.all_to_all(snapshots, "tm", split_axis=2, concat_axis=0, tiled=True))
    cell_count = spectra.shape[4]
    spectra = spectra.reshape(K, 2 * NB * 3 * cell_count)
    tm_total = lax.axis_size("tm")
    space_total = lax.axis_size("space")
    device_total = tm_total * space_total
    weight_scale = 1.0 / math.sqrt(3.0 * cell_count * device_total)
    local_w = (
        lax.dynamic_slice_in_dim(cell_weights, lax.axis_index("tm") * cell_count, cell_count, 0)
        * weight_scale
    )
    weight_rows = jnp.tile(local_w, 3)
    flat_slots = owner_slots.reshape(-1)
    my_rows = flat_slots.shape[0] // device_total
    return lax.psum_scatter(
        blocked(flat_slots, my_rows, spectra, weight_rows, triads),
        ("tm", "space"),
        scatter_dimension=0,
        tiled=True,
    )


def solution(mesh):
    placed = (P("tm", None, "space"), P("space"), P(), P())
    return jax.shard_map(
        shards, mesh=mesh, in_specs=placed, out_specs=P(("tm", "space"), None), check_vma=False
    )
```

profile of v0, /device:TPU:0, one launch (start us, length us, event | category | flops | bytes accessed | tf_op | source)
XLA Modules:
  0.0 327.5 jit_solution(2348501136595664732)
XLA Ops:
  6.5 7.7 %copy.36 = bf16[512,3,1024]{0,1,2:T(4,128)(2,1)} copy(bf16[512,3,1024]{2,0,1:T(8,128)(2,1)} %param.8) | data formatting | bytes 6291456 | tf_op args[0]
  14.2 7.4 %all-to-all-start = ((bf16[512,3,1024]{0,1,2:T(4,128)(2,1)}), bf16[512,3,1024]{0,1,2:T(4,128)(2,1)}, u32[]{:S(2)}, u32[]{:S(2)}) async-start(bf16[512,3,1024]{0,1,2:T(4,128)(2,1)} %copy.36), calls=%async_computation | async-start | bytes 8388608 | tf_op jit(solution)/shard_map/all_to_all | solution.py:81
  22.7 0.8 dynamic-slice_multiply_fusion
  23.5 91.4 %all-to-all-done = bf16[512,3,1024]{0,1,2:T(4,128)(2,1)} async-done(((bf16[512,3,1024]{0,1,2:T(4,128)(2,1)}), bf16[512,3,1024]{0,1,2:T(4,128)(2,1)}, u32[]{:S(2)}, u32[]{:S(2)}) %all-to-all-start) | async-done | bytes 3145760 | tf_op jit(solution)/shard_map/all_to_all | solution.py:81
  114.9 4.5 %copy.54 = bf16[512,3,8,128]{0,2,3,1:T(8,128)(2,1)S(1)} copy(bf16[512,3,8,128]{0,1,3,2:T(4,128)(2,1)} %bitcast) | data formatting | bytes 6291456 | tf_op jit(solution)/shard_map/all_to_all | solution.py:81
  119.4 3.4 %reshape.253 = bf16[16,256,384]{1,0,2:T(8,128)(2,1)} reshape(bf16[8,512,3,128]{1,0,3,2:T(8,128)(2,1)S(1)} %bitcast.74) | data formatting | bytes 6291456 | tf_op jit(solution)/shard_map/reshape | solution.py:27
  122.7 4.2 %fusion.12 = bf16[256,16,384]{2,0,1:T(8,128)(2,1)S(1)} fusion(bf16[256,256,1]{1,0,2:T(8,128)(2,1)S(1)} %reshape.310, bf16[16,256,384]{1,0,2:T(8,128)(2,1)} %reshape.253), kind=kOutput, calls=%fused_computation.46 | convolution fusion | flops 806879232 | bytes 6422528 | tf_op jit(solution)/shard_map/jn,bnc->jbc/dot_general | solution.py:28
  127.0 3.5 %copy.39 = bf16[256,16,384]{2,1,0:T(8,128)(2,1)} copy(bf16[256,16,384]{2,0,1:T(8,128)(2,1)S(1)} %fusion.12) | data formatting | bytes 6291456 | tf_op jit(solution)/shard_map/convert_element_type | solution.py:31
  130.5 4.2 %reshape_reshape.7 = bf16[128,12288]{1,0:T(8,128)(2,1)S(1)} reshape(bf16[256,16,384]{2,1,0:T(8,128)(2,1)} %copy.39) | data formatting | bytes 6291456 | tf_op jit(solution)/shard_map/reshape;reshape | solution.py:83
  134.7 60.4 %while.11 = (s32[]{:T(128)}, f32[2,64,512]{2,1,0:T(8,128)}, s32[2,64]{1,0:T(2,128)S(1)}, s32[64,3]{1,0:T(8,128)S(1)}, bf16[128,12288]{1,0:T(8,128)(2,1)S(1)}, /*index=5*/f32[128]{0:T(128)S(1)}, s32[]{:T(128)}) while((s32[]{:T(128)}, f32[2,64,512]{2,1,0:T(8,128)}, s32[2,64]{1,0:T(2,128)S(1)}, s32[64,3]{1,0:T(8,128)S(1)}, ...), condition=%wide.region_1.3_spmd.clone, body=%wide.region_0.2_spmd.clone.sunk | while | flops 61446336 | bytes 69630632 | solution.py:77
  134.7 0.6 gather_fusion
  135.7 2.7 gather_fusion.1
  138.4 1.7 select_convert_fusion.4
  140.0 2.2 copy.61
  142.3 2.7 gather_fusion.2
  145.0 1.7 select_convert_fusion.5
  146.7 0.6 copy.62
  147.2 1.3 copy-done
  148.5 1.7 multiply_convert_fusion.5
  150.2 2.7 gather_fusion.3
  152.9 1.6 broadcast_select_fusion.5
  154.8 0.9 copy-done.1
  155.9 2.9 fusion.30
  158.9 1.1 fusion.31
  160.0 1.3 copy.64
  161.3 1.3 copy.65
  162.6 0.8 copy.66
  163.4 1.6 constant_dynamic-update-slice_fusion.2
  164.9 0.6 gather_fusion
  165.9 2.7 gather_fusion.1
  168.6 1.7 select_convert_fusion.4
  170.2 2.2 copy.61
  172.5 2.7 gather_fusion.2
  175.2 1.7 select_convert_fusion.5
  176.9 0.6 copy.62
  177.4 1.3 copy-done
  178.7 1.7 multiply_convert_fusion.5
  180.4 2.7 gather_fusion.3
  183.1 1.6 broadcast_select_fusion.5
  185.0 0.9 copy-done.1
  186.1 2.9 fusion.30
  189.1 1.1 fusion.31
  190.2 1.3 copy.64
  191.5 1.3 copy.65
  192.8 0.8 copy.66
  193.6 1.6 constant_dynamic-update-slice_fusion.2
  195.1 124.2 %all-reduce.3.cloned.1.call-done = f32[128,512]{1,0:T(8,128)} async-done(((f32[128,512]{1,0:T(8,128)}), f32[128,512]{1,0:T(8,128)}) %all-reduce.3.cloned.1.call-update) | async-done | bytes 262160
  319.4 1.3 constant_dynamic-slice_fusion.1
  (55 shorter events, 2.9 us)
Async XLA Ops:
  14.2 8.4 %copy-start.4 = (s32[64,3]{0,1:T(4,128)S(1)}, s32[64,3]{0,1:T(4,128)}, u32[]{:S(2)}) copy-start(s32[64,3]{0,1:T(4,128)} %param.10) | copy-start | bytes 2308
  14.2 8.5 %copy-start.3 = (s32[8,16]{1,0:T(8,128)S(1)}, s32[8,16]{1,0:T(8,128)}, u32[]{:S(2)}) copy-start(s32[8,16]{1,0:T(8,128)} %param.11) | copy-start | bytes 1540
  14.2 100.7 %all-to-all-start = ((bf16[512,3,1024]{0,1,2:T(4,128)(2,1)}), bf16[512,3,1024]{0,1,2:T(4,128)(2,1)}, u32[]{:S(2)}, u32[]{:S(2)}) async-start(bf16[512,3,1024]{0,1,2:T(4,128)(2,1)} %copy.36), calls=%async_computation | async-start | bytes 8388608 | tf_op jit(solution)/shard_map/all_to_all | solution.py:81
  21.6 297.7 %all-reduce.3.cloned.1.call-start = ((), (), s32[]{:S(2)}) async-start(), calls=%async_computation.1 | async-start | bytes 524288
  146.6 1.9 copy-start
  154.5 1.1 copy-start.1
  154.5 1.4 copy-start.2
  176.8 1.9 copy-start
  184.7 1.1 copy-start.1
  184.7 1.4 copy-start.2
Sparse Core Ops, SparseCore 0:
  195.3 124.0 all-reduce.2
where the time goes:
time: 329 us; the launch traced here: 328 us
  waiting for transfers between devices  216 us (66%)
  local copies, waits for them, and re-layouts  63.2 us (19%)
  other arithmetic  17.4 us (5%)
  between operations  13.5 us (4%)
  matrix products  10.1 us (3%)
  starting transfers between devices  7.45 us (2%)
    unnamed x2, waiting for transfers between devices  124 us
    all_to_all x1, waiting for transfers between devices, shards(): lax.all_to_all(snapshots, 'tm', split_axis=2, concat_axis=0, tiled=True)  91.4 us
    while x18, local copies, waits for them, and re-layouts  10.8 us
    unnamed x7, local copies, waits for them, and re-layouts  9.08 us
    all_to_all x1, starting transfers between devices, shards(): lax.all_to_all(snapshots, 'tm', split_axis=2, concat_axis=0, tiled=True)  7.41 us
  transfers between devices with their start and end apart: 2, of which 2 were waited for; matrix products, arithmetic and copies ran while one was open for 1% of the time, Pallas kernels for 0%

commit v1 on v0

v1 whole, which is shorter than its diff:
```python
import functools
import math

import jax
import jax.numpy as jnp
import ml_dtypes
import numpy as np
from jax import lax
from jax.experimental import pallas as pl
from jax.experimental.pallas import tpu as pltpu
from jax.sharding import PartitionSpec as P

NB = 16
NT = 256
K = 128
GROUP = 8
LANES = 128
MESH = pl.DeviceIdType.MESH


def spectral_table():
    sample = np.arange(NT)
    freq_bins = np.arange(K)
    angles = 2.0 * math.pi / NT * (freq_bins[:, None] * sample[None, :] % NT)
    window = 0.5 - 0.5 * np.cos(2.0 * math.pi / NT * sample)
    scale = math.sqrt(8.0 / (3.0 * NT))
    rows = np.stack(
        [scale * window * np.cos(angles), -scale * window * np.sin(angles)], axis=1
    )
    return rows.reshape(2 * K, NT).astype(np.float32).astype(ml_dtypes.bfloat16)


def kernel(
    n,
    ns,
    weight_scale,
    snap,
    table,
    weights,
    freqs,
    out,
    recv,
    rows,
    spec,
    narrow,
    acc,
    part,
    summed,
    last,
    send_sem,
    recv_sem,
    own_sem,
    send1,
    recv1,
    send2,
    recv2,
):
    comps, times = snap.shape[0], snap.shape[1]
    me = lax.axis_index("tm")
    col = lax.axis_index("space")

    barrier = pltpu.get_barrier_semaphore()

    def greet_tm(off, carry):
        pl.semaphore_signal(
            barrier, inc=1, device_id=(lax.rem(me + off, n), col), device_id_type=MESH
        )
        return carry

    lax.fori_loop(1, n, greet_tm, 0)
    for off in range(1, ns):
        pl.semaphore_signal(
            barrier, inc=1, device_id=(me, lax.rem(col + off, ns)), device_id_type=MESH
        )
    pl.semaphore_wait(barrier, n - 1 + ns - 1)

    def exchange(c, off):
        peer = lax.rem(me + off, n)
        return pltpu.make_async_remote_copy(
            src_ref=snap.at[c, :, pl.ds(pl.multiple_of(peer * LANES, LANES), LANES)],
            dst_ref=recv.at[c, pl.ds(pl.multiple_of(me * times, 16), times), :],
            send_sem=send_sem.at[c, off],
            recv_sem=recv_sem.at[c, off],
            device_id=(peer, col),
            device_id_type=MESH,
        )

    def own(c):
        return pltpu.make_async_copy(
            snap.at[c, :, pl.ds(pl.multiple_of(me * LANES, LANES), LANES)],
            recv.at[c, pl.ds(pl.multiple_of(me * times, 16), times), :],
            own_sem.at[c],
        )

    for c in range(comps):

        def begin(off, carry, c=c):
            exchange(c, off).start()
            return carry

        lax.fori_loop(1, n, begin, 0)
        own(c).start()

    w_row = weights[pl.ds(me, 1), :] * weight_scale
    lane = lax.broadcasted_iota(jnp.int32, (2 * NB, 2 * LANES), 1)
    lane_group = lax.rem(lane, LANES) // NB
    low = lax.broadcasted_iota(jnp.int32, (NB, LANES), 1) < LANES // 2
    groups = freqs.shape[1] // GROUP
    per_owner = groups // n

    def dft(c, b):
        x = recv[c, pl.ds(pl.multiple_of(b * NT, NT), NT), :]
        y = jnp.dot(table[...], x, preferred_element_type=jnp.float32)
        rows[pl.ds(b, 2 * K, stride=NB), :] = y

    def regroup(k, carry):
        both = rows[pl.ds(pl.multiple_of(k * 2 * NB, 2 * NB), 2 * NB), :].astype(jnp.bfloat16)
        narrow[k] = both
        spec[k] = both.astype(jnp.float32)
        return carry

    def gram_group(c, g):
        owner = g // per_owner
        half = lax.rem(g, per_owner)
        prods, c_re, c_im = [], [], []
        for s in range(GROUP):
            place = g * GROUP + s
            a = spec[freqs[0, place]]
            b2 = spec[freqs[1, place]]
            c2 = narrow[freqs[2, place]]
            re = (a[:NB] * b2[:NB] - a[NB:] * b2[NB:]) * w_row
            im = (a[:NB] * b2[NB:] + a[NB:] * b2[:NB]) * w_row
            prods += [re.astype(jnp.bfloat16), im.astype(jnp.bfloat16)]
            c_re.append(c2[:NB])
            c_im.append(c2[NB:])
        left = jnp.concatenate(prods, axis=0)
        right = jnp.concatenate(c_re + c_im, axis=0)
        gram = lax.dot_general(
            left, right, (((1,), (1,)), ((), ())), preferred_element_type=jnp.float32
        )
        diag = gram[: 2 * NB]
        for s in range(1, GROUP):
            diag = jnp.where(lane_group == s, gram[2 * NB * s : 2 * NB * (s + 1)], diag)
        real = diag[:NB, :LANES] + diag[NB:, LANES:]
        imag = diag[:NB, LANES:] - diag[NB:, :LANES]
        half_turn = LANES // 2
        first = jnp.where(low, real, pltpu.roll(imag, half_turn, 1))
        second = jnp.where(low, pltpu.roll(real, half_turn, 1), imag)
        if c == 0:
            acc[2 * half, owner] = first
            acc[2 * half + 1, owner] = second
        else:
            acc[2 * half, owner] += first
            acc[2 * half + 1, owner] += second

    for c in range(comps):
        own(c).wait()
        if times % NT == 0:

            def transform(i, carry, c=c):
                dft(c, me * (times // NT) + i)
                return carry

            lax.fori_loop(0, times // NT, transform, 0)

            def arrive(off, carry, c=c):
                exchange(c, off).wait_recv()
                src = lax.rem(me - off + n, n)
                for i in range(times // NT):
                    dft(c, src * (times // NT) + i)
                return carry

            lax.fori_loop(1, n, arrive, 0)
        else:

            def arrive(off, carry, c=c):
                exchange(c, off).wait_recv()
                return carry

            lax.fori_loop(1, n, arrive, 0)

            def transform(b, carry, c=c):
                dft(c, b)
                return carry

            lax.fori_loop(0, NB, transform, 0)

        lax.fori_loop(0, K, regroup, 0, unroll=4)

        def grams(g, carry, c=c):
            gram_group(c, g)
            return carry

        lax.fori_loop(0, groups, grams, 0)

    def across(off):
        peer = lax.rem(col + off, ns)
        return pltpu.make_async_remote_copy(
            src_ref=acc.at[peer],
            dst_ref=part.at[off - 1],
            send_sem=send1.at[off - 1],
            recv_sem=recv1.at[off - 1],
            device_id=(me, peer),
            device_id_type=MESH,
        )

    for off in range(1, ns):
        across(off).start()
    for off in range(1, ns):
        across(off).wait_recv()
    total = acc[col]
    for off in range(1, ns):
        total = total + part[off - 1]
    summed[...] = total

    def along(off):
        peer = lax.rem(me + off, n)
        return pltpu.make_async_remote_copy(
            src_ref=summed.at[peer],
            dst_ref=last.at[off],
            send_sem=send2.at[off],
            recv_sem=recv2.at[off],
            device_id=(peer, col),
            device_id_type=MESH,
        )

    def begin2(off, carry):
        along(off).start()
        return carry

    lax.fori_loop(1, n, begin2, 0)

    def add2(off, total):
        along(off).wait_recv()
        return total + last[off]

    out[...] = lax.fori_loop(1, n, add2, summed[me])

    for off in range(1, ns):
        across(off).wait_send()

    def drain(off, carry):
        for c in range(comps):
            exchange(c, off).wait_send()
        along(off).wait_send()
        return carry

    lax.fori_loop(1, n, drain, 0)


def shards(n, ns, snapshots, cell_weights, triads, owner_slots):
    times, comps, cells = snapshots.shape
    owners, slot_count = owner_slots.shape
    weight_scale = 1.0 / math.sqrt(comps * cells * ns)
    vmem = pl.BlockSpec(memory_space=pltpu.VMEM)
    smem = pl.BlockSpec(memory_space=pltpu.SMEM)
    anywhere = pl.BlockSpec(memory_space=pl.ANY)
    sem = pltpu.SemaphoreType.DMA
    tile = pl.pallas_call(
        functools.partial(kernel, n, ns, weight_scale),
        out_shape=jax.ShapeDtypeStruct((NB, LANES), jnp.float32),
        in_specs=[anywhere, vmem, vmem, smem],
        out_specs=vmem,
        scratch_shapes=[
            pltpu.VMEM((comps, NB * NT, LANES), jnp.bfloat16),
            pltpu.VMEM((2 * K * NB, LANES), jnp.float32),
            pltpu.VMEM((K, 2 * NB, LANES), jnp.float32),
            pltpu.VMEM((K, 2 * NB, LANES), jnp.bfloat16),
            pltpu.VMEM((ns, n, NB, LANES), jnp.float32),
            pltpu.VMEM((ns - 1, n, NB, LANES), jnp.float32),
            pltpu.VMEM((n, NB, LANES), jnp.float32),
            pltpu.VMEM((n, NB, LANES), jnp.float32),
            sem((comps, n)),
            sem((comps, n)),
            sem((comps,)),
            sem((ns - 1,)),
            sem((ns - 1,)),
            sem((n,)),
            sem((n,)),
        ],
        compiler_params=pltpu.CompilerParams(
            collective_id=0, has_side_effects=True, vmem_limit_bytes=40 * 1024 * 1024
        ),
    )(
        snapshots.transpose(1, 0, 2),
        jnp.asarray(spectral_table()),
        cell_weights.reshape(n, LANES),
        jnp.take(triads.T, jnp.maximum(owner_slots, 0).reshape(-1), axis=1, mode="clip"),
    )
    mine = slot_count // ns
    flat = tile.reshape(NB, 2, mine, NB).transpose(2, 1, 0, 3).reshape(mine, 2 * NB * NB)
    my_slots = lax.dynamic_slice(
        owner_slots, (lax.axis_index("tm"), lax.axis_index("space") * mine), (1, mine)
    ).reshape(mine, 1)
    return jnp.where(my_slots >= 0, flat, 0.0)


def solution(mesh):
    placed = (P("tm", None, "space"), P("space"), P(), P())
    n, ns = mesh.shape["tm"], mesh.shape["space"]
    return jax.shard_map(
        functools.partial(shards, n, ns),
        mesh=mesh,
        in_specs=placed,
        out_specs=P(("tm", "space"), None),
        check_vma=False,
    )
```

time: 329 us -> 97.4 us (0.30)
  waiting for transfers between devices: 216 us -> 0 us
  Pallas kernels: 0 us -> 89.7 us
  local copies, waits for them, and re-layouts: 63.2 us -> 5.26 us
  other arithmetic: 17.4 us -> 2.14 us
  between operations: 13.5 us -> 0.03 us
  matrix products: 10.1 us -> 0 us
  starting transfers between devices: 7.45 us -> 0 us
    unnamed x2 -> x0, waiting for transfers between devices: 124 us -> none
    all_to_all x1 -> x0, waiting for transfers between devices: 91.4 us -> none  [shards(): lax.all_to_all(snapshots, 'tm', split_axis=2, concat_axis=0, tiled=True)]
    pallas_call x0 -> x1, Pallas kernels: none -> 89.7 us  [shards(): pl.pallas_call(functools.partial(kernel, n, ns, weight_scale), out_shape=...]
    gather x8 -> x2, local copies, waits for them, and re-layouts: 17.3 us -> 0.7 us  [shards(): jnp.take(triads.T, jnp.maximum(owner_slots, 0).reshape(-1), axis=1, mode=...]
    while x18 -> x0, local copies, waits for them, and re-layouts: 10.8 us -> none
    dot_general x3 -> x0, matrix products: 10.1 us -> none  [the longest x2 5.9 us: triad_terms(): jnp.einsum('trbc,tsdc->trbsd', product, third_spec, preferred_element_typ...]
    all_to_all x1 -> x0, starting transfers between devices: 7.41 us -> none  [shards(): lax.all_to_all(snapshots, 'tm', split_axis=2, concat_axis=0, tiled=True)]
    convert_element_type x6 -> x0, other arithmetic: 6.74 us -> none  [the longest x2 3.36 us: triad_terms(): second_spec = jnp.take(spectra, triad_freqs[:, 1], axis=0).reshape(count,...]
  transfers between devices with their start and end apart: 2 -> 0, of which waited for: 2 -> 0; matrix products, arithmetic and copies ran while one was open for 1% -> 0% of each run, Pallas kernels for 0% -> 0%
where the time goes in v1:
time: 97.4 us; the launch traced here: 97.1 us
  Pallas kernels  89.7 us (92%)
  local copies, waits for them, and re-layouts  5.26 us (5%)
  other arithmetic  2.14 us (2%)
    pallas_call x1, Pallas kernels, shards(): pl.pallas_call(functools.partial(kernel, n, ns, weight_scale), out_shape=...  89.7 us
    unnamed x7, local copies, waits for them, and re-layouts  4.27 us

profile of v1, /device:TPU:0, one launch (start us, length us, event | category | flops | bytes accessed | tf_op | source)
XLA Modules:
  0.0 97.1 jit_solution(9721842767064481788)
XLA Ops:
  0.0 0.8 copy.6
  0.8 0.7 broadcast_maximum_fusion
  1.5 0.1 reshape.26
  1.6 0.6 gather_fusion
  2.2 0.1 copy.7
  2.3 0.0 copy-start
  2.3 1.9 %copy-done = bf16[512,3,1024]{2,0,1:T(8,128)(2,1)S(1)} copy-done((bf16[512,3,1024]{2,0,1:T(8,128)(2,1)S(1)}, bf16[512,3,1024]{2,0,1:T(8,128)(2,1)}, u32[]{:S(2)}) %copy-start) | copy-done | bytes 3145752
  4.2 0.0 copy-start.1
  4.2 0.9 copy-done.1
  5.1 0.0 copy-start.2
  5.1 0.7 copy-done.2
  5.8 89.7 %shard_map.55 = f32[16,128]{1,0:T(8,128)S(1)} custom-call(bf16[3,512,1024]{2,1,0:T(8,128)(2,1)S(1)} %bitcast.9, bf16[256,256]{1,0:T(8,128)(2,1)S(1)} %copy-done.1, f32[8,128]{1,0:T(8,128)S(1)} %bitcast.11, s32[3,128]{1,0:T(4,128)S(1)} %bitcast.10), custom_call_target="tpu_custom_call" | custom-call | tf_op jit(solution)/shard_map/pallas_call | solution.py:259
  95.5 0.1 reshape.22
  95.6 0.1 reshape.23
  95.7 0.8 compare_bitcast_fusion
  96.5 0.7 broadcast_select_fusion
  (2 shorter events, 0.0 us)
Async XLA Ops:
  2.3 1.9 %copy-start = (bf16[512,3,1024]{2,0,1:T(8,128)(2,1)S(1)}, bf16[512,3,1024]{2,0,1:T(8,128)(2,1)}, u32[]{:S(2)}) copy-start(bf16[512,3,1024]{2,0,1:T(8,128)(2,1)} %param.5) | copy-start | bytes 9437188
  4.2 0.9 copy-start.1
  5.1 0.7 copy-start.2
